TPU v7x, 512 devices: a whole 4x4x16 slice. The times are simulated.
512 devices in a mesh: pp: 32 (over x_hi, z), ep: 16 (over x_lo, y, core).
Axes of the slice: x: 4 (x_hi: 2, x_lo: 2; x = x_hi * 2 + x_lo), y: 4, z: 16, core: 2. Of those that a mesh axis runs over, the one named last changes fastest.
Arguments:
- section_out: bfloat16 [32768, 3584], P(('pp', 'ep')), may hold values from -6 to 6
- routes_fwd: int32 [32768, 1], P(('pp', 'ep')), may hold values from 0 to 1; in each aligned block of 64 rows (0 to 63, 64 to 127, ...) at most 32 rows name the same one
- gates_fwd: float32 [32768, 1], P(('pp', 'ep')), may hold values from 0.1 to 1
- cot_next: bfloat16 [32768, 3584], P(('pp', 'ep')), may hold values from -6 to 6
- routes_bwd: int32 [32768, 1], P(('pp', 'ep')), may hold values from 0 to 1; in each aligned block of 64 rows (0 to 63, 64 to 127, ...) at most 32 rows name the same one
- gates_bwd: float32 [32768, 1], P(('pp', 'ep')), may hold values from 0.1 to 1
- norm_gain: float32 [32, 3584], P('pp'), may hold values from 0.1 to 1.9
- saved_gate: bfloat16 [32, 512, 2048], P('pp', None, 'ep'), may hold values from -6 to 6
- saved_up: bfloat16 [32, 512, 2048], P('pp', None, 'ep'), may hold values from -6 to 6
- w_gate: bfloat16 [32, 3584, 2048], P('pp', None, 'ep'), may hold values from -0.09375 to 0.09375
- w_up: bfloat16 [32, 3584, 2048], P('pp', None, 'ep'), may hold values from -0.09375 to 0.09375
- w_down: bfloat16 [32, 2048, 3584], P('pp', 'ep'), may hold values from -0.1875 to 0.1875
Outputs:
- section_result: bfloat16 [32768, 3584], P(('pp', 'ep'))
- input_grad: bfloat16 [32768, 3584], P(('pp', 'ep'))
Inputs may be any that keep to these rules, and one draw needn't show every extreme that they name: `routes_fwd`: in the rows of one device each expert is named exactly 32 times. `routes_bwd`: as for routes_fwd.
All inputs are finite; a program needn't handle non-finite values.
Results may differ from a plain program's by a relative error of at most 0.0064.
Values may be sent and summed in bfloat16 or wider, within the bound.
A program may use at most 64 MiB of HBM per device.

v0:
```python
import jax
import jax.numpy as jnp
from jax import lax
from jax.sharding import PartitionSpec as P

EXPERTS = 2


EPS = 1e-06


def passed_along(value, axis, steps):
    count = lax.axis_size(axis)
    pairs = [(source, (source + steps) % count) for source in range(count)]
    return lax.ppermute(value, axis, pairs)


def slot_places(routes, experts, capacity):
    flat = routes.reshape(-1)
    onehot = (flat[:, None] == jnp.arange(experts, dtype=jnp.int32)[None, :]).astype(jnp.int32)
    before = jnp.cumsum(onehot, axis=0) - onehot
    slot = jnp.sum(before * onehot, axis=1)
    return flat * capacity + slot


def normalize(values, gain):
    floats = values.astype(jnp.float32)
    scale = lax.rsqrt(jnp.mean(floats * floats, axis=-1, keepdims=True) + EPS)
    return (floats * scale * gain).astype(jnp.bfloat16)


def dispatch(rows, places, experts, capacity):
    buffer = jnp.zeros((experts * capacity, rows.shape[-1]), rows.dtype)
    buffer = buffer.at[places].set(rows)
    return buffer.reshape(experts, capacity, rows.shape[-1])


def contract_last(left, right):
    return lax.dot_general(
        left, right, (((1,), (1,)), ((), ())), preferred_element_type=jnp.float32
    )


def local(
    section_out,
    routes_fwd,
    gates_fwd,
    cot_next,
    routes_bwd,
    gates_bwd,
    norm_gain,
    saved_gate,
    saved_up,
    w_gate,
    w_up,
    w_down,
):
    devices = lax.axis_size("ep")
    count, picks = routes_fwd.shape
    width = section_out.shape[1]
    capacity = count * picks // EXPERTS
    group = devices // EXPERTS
    gain = norm_gain[0]
    gate_cols = w_gate[0]
    up_cols = w_up[0]
    down_rows = w_down[0]
    held_gate = saved_gate[0].astype(jnp.float32)
    held_up = saved_up[0].astype(jnp.float32)
    arrived = passed_along(section_out, "pp", 1)
    upstream = passed_along(cot_next, "pp", -1)
    places_a = slot_places(routes_fwd, EXPERTS, capacity)
    places_b = slot_places(routes_bwd, EXPERTS, capacity)
    hidden_a = normalize(arrived, gain)
    buffer_a = dispatch(jnp.repeat(hidden_a, picks, axis=0), places_a, EXPERTS, capacity)
    send_a = jnp.repeat(buffer_a, group, axis=0)
    grad_out = upstream.astype(jnp.float32)
    scaled = (gates_bwd[:, :, None] * grad_out[:, None, :]).astype(jnp.bfloat16)
    buffer_c = dispatch(scaled.reshape(count * picks, width), places_b, EXPERTS, capacity)
    send_c = jnp.repeat(buffer_c, group, axis=0)
    came_a, came_c = (
        lax.all_to_all(send_a, "ep", split_axis=0, concat_axis=0, tiled=True),
        lax.all_to_all(send_c, "ep", split_axis=0, concat_axis=0, tiled=True),
    )
    flat = came_a.reshape(-1, width)
    gate_act = jnp.dot(flat, gate_cols, preferred_element_type=jnp.float32)
    up_act = jnp.dot(flat, up_cols, preferred_element_type=jnp.float32)
    inner = (gate_act * jax.nn.sigmoid(gate_act) * up_act).astype(jnp.bfloat16)
    output = jnp.dot(inner, down_rows, preferred_element_type=jnp.float32).astype(jnp.bfloat16)
    back_a = lax.all_to_all(
        output.reshape(came_a.shape), "ep", split_axis=0, concat_axis=0, tiled=True
    )
    flat = came_c.reshape(-1, width)
    inner_grad = contract_last(flat, down_rows)
    sigma = jax.nn.sigmoid(held_gate)
    gate_grad = (inner_grad * held_up * sigma * (1.0 + held_gate * (1.0 - sigma))).astype(
        jnp.bfloat16
    )
    up_grad = (inner_grad * held_gate * sigma).astype(jnp.bfloat16)
    total = contract_last(gate_grad, gate_cols) + contract_last(up_grad, up_cols)
    back_b = lax.all_to_all(
        total.astype(jnp.bfloat16).reshape(came_c.shape),
        "ep",
        split_axis=0,
        concat_axis=0,
        tiled=True,
    )

    def combine_back(returned, places):
        floats = returned.astype(jnp.float32).reshape(EXPERTS, group, capacity, width)
        summed = jnp.sum(floats, axis=1).reshape(EXPERTS * capacity, width)
        return summed[places]

    picked_a = combine_back(back_a, places_a).reshape(count, picks, width)
    result = arrived.astype(jnp.float32) + jnp.sum(picked_a * gates_fwd[:, :, None], axis=1)
    picked_b = combine_back(back_b, places_b).reshape(count, picks, width)
    grad_in = jnp.sum(picked_b, axis=1)
    return (result.astype(jnp.bfloat16), grad_in.astype(jnp.bfloat16))


def solution(mesh):
    in_specs = (
        P(("pp", "ep"), None),
        P(("pp", "ep"), None),
        P(("pp", "ep"), None),
        P(("pp", "ep"), None),
        P(("pp", "ep"), None),
        P(("pp", "ep"), None),
        P("pp", None),
        P("pp", None, "ep"),
        P("pp", None, "ep"),
        P("pp", None, "ep"),
        P("pp", None, "ep"),
        P("pp", "ep", None),
    )
    out_specs = (P(("pp", "ep"), None), P(("pp", "ep"), None))
    return jax.shard_map(local, mesh=mesh, in_specs=in_specs, out_specs=out_specs, check_vma=False)
```

profile of v0, /device:TPU:25, one launch (start us, length us, event | category | flops | bytes accessed | tf_op | source)
XLA Modules:
  0.0 271.5 jit_solution(2199248324704783356)
XLA Ops:
  0.6 3.7 %collective-permute-start = (bf16[64,3584]{1,0:T(8,128)(2,1)}, bf16[64,3584]{1,0:T(8,128)(2,1)S(1)}, u32[]{:S(2)}, u32[]{:S(2)}) collective-permute-start(bf16[64,3584]{1,0:T(8,128)(2,1)} %param.12), channel_id=1, source_target_pairs={{0,16},{16,32},{32,48},{48,64},{64,80},{80,96},{96,112},{112,128},... | collective-permute-start | bytes 1376264 | tf_op jit(solution)/shard_map/ppermute | solution.py:15
  4.3 0.7 fusion.46
  5.2 0.8 reduce
  5.9 0.8 select_reduce_fusion.1
  6.8 0.7 fusion.47
  7.4 17.4 %collective-permute-done = bf16[64,3584]{1,0:T(8,128)(2,1)S(1)} collective-permute-done((bf16[64,3584]{1,0:T(8,128)(2,1)}, bf16[64,3584]{1,0:T(8,128)(2,1)S(1)}, u32[]{:S(2)}, u32[]{:S(2)}) %collective-permute-start) | collective-permute-done | bytes 458784 | tf_op jit(solution)/shard_map/ppermute | solution.py:15
  24.8 0.2 fusion.1
  25.0 1.5 scatter_custom_fusion
  26.5 2.2 broadcast_in_dim.4
  28.6 5.7 %all-to-all-start = ((bf16[16,32,3584]{2,1,0:T(8,128)(2,1)}), bf16[16,32,3584]{2,1,0:T(8,128)(2,1)}, u32[]{:S(2)}, u32[]{:S(2)}) async-start(bf16[16,32,3584]{2,1,0:T(8,128)(2,1)} %bitcast.70), calls=%async_computation | async-start | bytes 7340032 | tf_op jit(solution)/shard_map/all_to_all | solution.py:81
  34.4 4.0 %collective-permute-start.1 = (bf16[64,3584]{1,0:T(8,128)(2,1)S(1)}, bf16[64,3584]{1,0:T(8,128)(2,1)S(1)}, u32[]{:S(2)}, u32[]{:S(2)}) collective-permute-start(bf16[64,3584]{1,0:T(8,128)(2,1)S(1)} %copy-done.8), channel_id=1, source_target_pairs={{0,496},{16,0},{32,16},{48,32},{64,48},{80,64},{96,80},{112,96},{1... | collective-permute-start | bytes 1376264 | tf_op jit(solution)/shard_map/ppermute | solution.py:15
  38.5 0.2 select_reduce_fusion
  38.7 9.4 %collective-permute-done.1 = bf16[64,3584]{1,0:T(8,128)(2,1)S(1)} collective-permute-done((bf16[64,3584]{1,0:T(8,128)(2,1)S(1)}, bf16[64,3584]{1,0:T(8,128)(2,1)S(1)}, u32[]{:S(2)}, u32[]{:S(2)}) %collective-permute-start.1) | collective-permute-done | bytes 458784 | tf_op jit(solution)/shard_map/ppermute | solution.py:15
  48.1 1.4 scatter_custom_fusion.1
  49.5 38.3 %all-to-all-done = bf16[16,32,3584]{2,1,0:T(8,128)(2,1)} async-done(((bf16[16,32,3584]{2,1,0:T(8,128)(2,1)}), bf16[16,32,3584]{2,1,0:T(8,128)(2,1)}, u32[]{:S(2)}, u32[]{:S(2)}) %all-to-all-start) | async-done | bytes 3670048 | tf_op jit(solution)/shard_map/all_to_all | solution.py:81
  87.8 2.3 broadcast_in_dim.5
  90.1 5.4 %all-to-all-start.2 = ((bf16[16,32,3584]{2,1,0:T(8,128)(2,1)}), bf16[16,32,3584]{2,1,0:T(8,128)(2,1)}, u32[]{:S(2)}, u32[]{:S(2)}) async-start(bf16[16,32,3584]{2,1,0:T(8,128)(2,1)} %bitcast.72), calls=%async_computation.2 | async-start | bytes 7340032 | tf_op jit(solution)/shard_map/all_to_all | solution.py:82
  95.5 3.2 %fusion.13 = f32[512,128]{1,0:T(8,128)S(1)} fusion(bf16[512,3584]{1,0:T(8,128)(2,1)} %bitcast.5, bf16[1,3584,128]{2,1,0:T(8,128)(2,1)S(1)} %copy-done.2), kind=kOutput, calls=%fused_computation.24 | convolution fusion | flops 469762048 | bytes 4849664 | tf_op jit(solution)/shard_map/dot_general | solution.py:85
  98.7 7.8 %convolution_convert_fusion = bf16[512,3584]{1,0:T(8,128)(2,1)} fusion(bf16[512,3584]{1,0:T(8,128)(2,1)} %bitcast.5, bf16[1,128,3584]{2,1,0:T(8,128)(2,1)S(1)} %copy-done.1, bf16[1,3584,128]{2,1,0:T(8,128)(2,1)S(1)} %copy-done, f32[512,128]{1,0:T(8,128)S(1)} %fusion.13), kind=kOutput, calls=%fused_computation.7 | convolution fusion | flops 941752320 | bytes 9437184 | tf_op jit(solution)/shard_map/dot_general | solution.py:88
  106.5 42.4 %all-to-all-done.2 = bf16[16,32,3584]{2,1,0:T(8,128)(2,1)} async-done(((bf16[16,32,3584]{2,1,0:T(8,128)(2,1)}), bf16[16,32,3584]{2,1,0:T(8,128)(2,1)}, u32[]{:S(2)}, u32[]{:S(2)}) %all-to-all-start.2) | async-done | bytes 3670048 | tf_op jit(solution)/shard_map/all_to_all | solution.py:82
  149.0 5.2 %all-to-all-start.1 = ((bf16[16,32,3584]{2,1,0:T(8,128)(2,1)}), bf16[16,32,3584]{2,1,0:T(8,128)(2,1)}, u32[]{:S(2)}, u32[]{:S(2)}) async-start(bf16[16,32,3584]{2,1,0:T(8,128)(2,1)} %bitcast.69), calls=%async_computation.1 | async-start | bytes 7340032 | tf_op jit(solution)/shard_map/all_to_all | solution.py:89
  154.2 3.2 %fusion.5 = f32[512,128]{1,0:T(8,128)S(1)} fusion(bf16[512,3584]{1,0:T(8,128)(2,1)} %bitcast.19, bf16[1,128,3584]{2,1,0:T(8,128)(2,1)S(1)} %copy-done.1), kind=kOutput, calls=%fused_computation.17 | convolution fusion | flops 469762048 | bytes 4849664 | tf_op jit(solution)/shard_map/dot_general | solution.py:39
  157.4 1.1 fusion.11
  158.5 3.0 %add_convert_fusion = bf16[512,3584]{1,0:T(8,128)(2,1)} fusion(f32[512,3584]{1,0:T(8,128)S(1)} %fusion.11, bf16[1,3584,128]{2,1,0:T(8,128)(2,1)S(1)} %copy-done, f32[512,128]{1,0:T(8,128)S(1)} %fusion.5, bf16[1,512,128]{2,1,0:T(8,128)(2,1)S(1)} %copy-done.3), kind=kOutput, calls=%fused_computation.6 | convolution fusion | flops 473890816 | bytes 12320768 | tf_op jit(solution)/shard_map/dot_general | solution.py:39
  161.6 46.1 %all-to-all-done.1 = bf16[16,32,3584]{2,1,0:T(8,128)(2,1)} async-done(((bf16[16,32,3584]{2,1,0:T(8,128)(2,1)}), bf16[16,32,3584]{2,1,0:T(8,128)(2,1)}, u32[]{:S(2)}, u32[]{:S(2)}) %all-to-all-start.1) | async-done | bytes 3670048 | tf_op jit(solution)/shard_map/all_to_all | solution.py:89
  207.7 5.2 %all-to-all-start.3 = ((bf16[16,32,3584]{2,1,0:T(8,128)(2,1)}), bf16[16,32,3584]{2,1,0:T(8,128)(2,1)}, u32[]{:S(2)}, u32[]{:S(2)}) async-start(bf16[16,32,3584]{2,1,0:T(8,128)(2,1)} %bitcast.71), calls=%async_computation.3 | async-start | bytes 7340032 | tf_op jit(solution)/shard_map/all_to_all | solution.py:100
  212.9 2.6 convert_reduce_fusion.1
  215.6 0.9 gather_fusion
  216.5 49.9 %all-to-all-done.3 = bf16[16,32,3584]{2,1,0:T(8,128)(2,1)} async-done(((bf16[16,32,3584]{2,1,0:T(8,128)(2,1)}), bf16[16,32,3584]{2,1,0:T(8,128)(2,1)}, u32[]{:S(2)}, u32[]{:S(2)}) %all-to-all-start.3) | async-done | bytes 3670048 | tf_op jit(solution)/shard_map/all_to_all | solution.py:100
  266.4 2.5 convert_reduce_fusion
  268.9 1.6 gather_fusion.1
  270.5 0.9 fusion.4
  (25 shorter events, 0.3 us)
Async XLA Ops:
  0.6 98.1 %copy-start = (bf16[1,3584,128]{2,1,0:T(8,128)(2,1)S(1)}, bf16[1,3584,128]{2,1,0:T(8,128)(2,1)}, u32[]{:S(2)}) copy-start(bf16[1,3584,128]{2,1,0:T(8,128)(2,1)} %param.22) | copy-start | bytes 2752516
  0.6 24.2 %collective-permute-start = (bf16[64,3584]{1,0:T(8,128)(2,1)}, bf16[64,3584]{1,0:T(8,128)(2,1)S(1)}, u32[]{:S(2)}, u32[]{:S(2)}) collective-permute-start(bf16[64,3584]{1,0:T(8,128)(2,1)} %param.12), channel_id=1, source_target_pairs={{0,16},{16,32},{32,48},{48,64},{64,80},{80,96},{96,112},{112,128},... | collective-permute-start | bytes 1376264 | tf_op jit(solution)/shard_map/ppermute | solution.py:15
  28.6 5.7 %copy-start.8 = (bf16[64,3584]{1,0:T(8,128)(2,1)S(1)}, bf16[64,3584]{1,0:T(8,128)(2,1)}, u32[]{:S(2)}) copy-start(bf16[64,3584]{1,0:T(8,128)(2,1)} %param.15) | copy-start | bytes 1376260
  28.6 9.7 %copy-start.5 = (s32[64,1]{0,1:T(1,128)S(1)}, s32[64,1]{0,1:T(1,128)}, u32[]{:S(2)}) copy-start(s32[64,1]{0,1:T(1,128)} %param.16) | copy-start | bytes 772
  28.6 19.5 %copy-start.6 = (f32[64,1]{0,1:T(1,128)S(1)}, f32[64,1]{0,1:T(1,128)}, u32[]{:S(2)}) copy-start(f32[64,1]{0,1:T(1,128)} %param.17) | copy-start | bytes 772
  28.6 59.2 %all-to-all-start = ((bf16[16,32,3584]{2,1,0:T(8,128)(2,1)}), bf16[16,32,3584]{2,1,0:T(8,128)(2,1)}, u32[]{:S(2)}, u32[]{:S(2)}) async-start(bf16[16,32,3584]{2,1,0:T(8,128)(2,1)} %bitcast.70), calls=%async_computation | async-start | bytes 7340032 | tf_op jit(solution)/shard_map/all_to_all | solution.py:81
  34.4 13.7 %collective-permute-start.1 = (bf16[64,3584]{1,0:T(8,128)(2,1)S(1)}, bf16[64,3584]{1,0:T(8,128)(2,1)S(1)}, u32[]{:S(2)}, u32[]{:S(2)}) collective-permute-start(bf16[64,3584]{1,0:T(8,128)(2,1)S(1)} %copy-done.8), channel_id=1, source_target_pairs={{0,496},{16,0},{32,16},{48,32},{64,48},{80,64},{96,80},{112,96},{1... | collective-permute-start | bytes 1376264 | tf_op jit(solution)/shard_map/ppermute | solution.py:15
  90.1 5.4 %copy-start.2 = (bf16[1,3584,128]{2,1,0:T(8,128)(2,1)S(1)}, bf16[1,3584,128]{2,1,0:T(8,128)(2,1)}, u32[]{:S(2)}) copy-start(bf16[1,3584,128]{2,1,0:T(8,128)(2,1)} %param.21) | copy-start | bytes 2752516
  90.1 58.8 %all-to-all-start.2 = ((bf16[16,32,3584]{2,1,0:T(8,128)(2,1)}), bf16[16,32,3584]{2,1,0:T(8,128)(2,1)}, u32[]{:S(2)}, u32[]{:S(2)}) async-start(bf16[16,32,3584]{2,1,0:T(8,128)(2,1)} %bitcast.72), calls=%async_computation.2 | async-start | bytes 7340032 | tf_op jit(solution)/shard_map/all_to_all | solution.py:82
  95.5 3.3 %copy-start.1 = (bf16[1,128,3584]{2,1,0:T(8,128)(2,1)S(1)}, bf16[1,128,3584]{2,1,0:T(8,128)(2,1)}, u32[]{:S(2)}) copy-start(bf16[1,128,3584]{2,1,0:T(8,128)(2,1)} %param.23) | copy-start | bytes 2752516
  149.0 58.7 %all-to-all-start.1 = ((bf16[16,32,3584]{2,1,0:T(8,128)(2,1)}), bf16[16,32,3584]{2,1,0:T(8,128)(2,1)}, u32[]{:S(2)}, u32[]{:S(2)}) async-start(bf16[16,32,3584]{2,1,0:T(8,128)(2,1)} %bitcast.69), calls=%async_computation.1 | async-start | bytes 7340032 | tf_op jit(solution)/shard_map/all_to_all | solution.py:89
  154.2 3.2 %copy-start.3 = (bf16[1,512,128]{2,1,0:T(8,128)(2,1)S(1)}, bf16[1,512,128]{2,1,0:T(8,128)(2,1)}, u32[]{:S(2)}) copy-start(bf16[1,512,128]{2,1,0:T(8,128)(2,1)} %param.19) | copy-start | bytes 393220
  154.2 3.2 %copy-start.4 = (bf16[1,512,128]{2,1,0:T(8,128)(2,1)S(1)}, bf16[1,512,128]{2,1,0:T(8,128)(2,1)}, u32[]{:S(2)}) copy-start(bf16[1,512,128]{2,1,0:T(8,128)(2,1)} %param.20) | copy-start | bytes 393220
  207.7 58.7 %all-to-all-start.3 = ((bf16[16,32,3584]{2,1,0:T(8,128)(2,1)}), bf16[16,32,3584]{2,1,0:T(8,128)(2,1)}, u32[]{:S(2)}, u32[]{:S(2)}) async-start(bf16[16,32,3584]{2,1,0:T(8,128)(2,1)} %bitcast.71), calls=%async_computation.3 | async-start | bytes 7340032 | tf_op jit(solution)/shard_map/all_to_all | solution.py:100
  216.4 54.1 %copy-start.7 = (f32[64,1]{0,1:T(1,128)S(1)}, f32[64,1]{0,1:T(1,128)}, u32[]{:S(2)}) copy-start(f32[64,1]{0,1:T(1,128)} %param.14) | copy-start | bytes 772
where the time goes:
time: 272 us; the launch traced here: 271 us
  waiting for transfers between devices  204 us (75%)
  starting transfers between devices  29.2 us (11%)
  matrix products  18.3 us (7%)
  other arithmetic  12.6 us (5%)
  local copies, waits for them, and re-layouts  6.95 us (3%)
    all_to_all x1, waiting for transfers between devices, local(): lax.all_to_all(total.astype(jnp.bfloat16).reshape(came_c.shape), 'ep', sp...  49.9 us
    all_to_all x1, waiting for transfers between devices, local(): lax.all_to_all(output.reshape(came_a.shape), 'ep', split_axis=0, concat_a...  46.1 us
    all_to_all x1, waiting for transfers between devices, local(): lax.all_to_all(send_c, 'ep', split_axis=0, concat_axis=0, tiled=True)  42.4 us
    all_to_all x1, waiting for transfers between devices, local(): lax.all_to_all(send_a, 'ep', split_axis=0, concat_axis=0, tiled=True)  38.3 us
    ppermute x2, waiting for transfers between devices, passed_along(): return lax.ppermute(value, axis, pairs)  26.8 us
    dot_general x1, matrix products, local(): jnp.dot(inner, down_rows, preferred_element_type=jnp.float32)  7.77 us
    ppermute x2, starting transfers between devices, passed_along(): return lax.ppermute(value, axis, pairs)  7.64 us
    dot_general x3, matrix products, contract_last(): lax.dot_general(left, right, (((1,), (1,)), ((), ())), preferred_element_...  7.36 us
  transfers between devices with their start and end apart: 6, of which 6 were waited for; matrix products, arithmetic and copies ran while one was open for 10% of the time, Pallas kernels for 0%

commit v1 on v0

v1 whole, which is shorter than its diff:
```python
import functools

import jax
import jax.numpy as jnp
from jax import lax
from jax.experimental import pallas as pl
from jax.experimental.pallas import tpu as pltpu
from jax.sharding import PartitionSpec as P

EXPERTS = 2
RING = 4
CORES = 2
EPS = 1e-06
CHUNKS = 7
START = 11
MESH = pl.DeviceIdType.MESH


def kernel(
    section_out,
    cot_next,
    routes_fwd,
    gates_fwd,
    routes_bwd,
    gates_bwd,
    norm_gain,
    saved_gate,
    saved_up,
    w_gate,
    w_up,
    w_down,
    result,
    grad_in,
    arr,
    disp,
    rows,
    gate_up,
    down,
    held_gate,
    held_up,
    pick,
    unpick,
    factor,
    row_gate,
    gate_out,
    act,
    squares,
    inner,
    back_act,
    back_inner,
    part,
    far_send,
    far_recv,
    near_send,
    near_recv,
    home_send,
    home,
    out_buf,
    load_sem,
    core_send,
    core_recv,
    pp_send,
    pp_recv,
    x_send,
    x_recv,
    y_send,
    y_recv,
    far_send_sem,
    far_recv_sem,
    near_send_sem,
    near_recv_sem,
    home_send_sem,
    home_recv_sem,
    gate_send_sem,
    gate_recv_sem,
    out_sem,
):
    count = section_out.shape[0]
    width = section_out.shape[1]
    cap = count // EXPERTS
    unit = w_gate.shape[2]
    units = unit * CORES
    cw = width // CHUNKS
    total = EXPERTS * RING * cap
    steps = 2 * CHUNKS
    f32, bf16 = jnp.float32, jnp.bfloat16

    me_pp = lax.axis_index("pp")
    me = lax.axis_index("ep")
    n_pp = lax.axis_size("pp")
    plane = me // (RING * CORES)
    other = 1 - plane
    y = (me // CORES) % RING
    core = me % CORES

    def in_ring(at):
        return {"ep": plane * (RING * CORES) + at * CORES + core}

    y_up = lax.rem(y + 1, RING)
    y_far = lax.rem(y + 2, RING)
    y_down = lax.rem(y + 3, RING)
    up = in_ring(y_up)
    dn = in_ring(y_down)
    across = {"ep": other * (RING * CORES) + y * CORES + core}
    twin = {"ep": plane * (RING * CORES) + y * CORES + (1 - core)}
    after = {"pp": lax.rem(me_pp + 1, n_pp)}
    before = {"pp": lax.rem(me_pp + n_pp - 1, n_pp)}

    own_lane = pl.multiple_of(core * unit, unit)

    def load(src, dst, at):
        return pltpu.make_async_copy(src, dst, load_sem.at[at])

    loads = [
        load(w_gate.at[0], gate_up.at[:, pl.ds(own_lane, unit)], 0),
        load(w_up.at[0], gate_up.at[:, pl.ds(pl.multiple_of(units + core * unit, unit), unit)], 1),
        load(w_down.at[0], down.at[pl.ds(own_lane, unit)], 2),
        load(saved_gate.at[:, core], held_gate.at[:, :, pl.ds(own_lane, unit)], 3),
        load(saved_up.at[:, core], held_up.at[:, :, pl.ds(own_lane, unit)], 4),
    ]
    for one in loads:
        one.start()

    barrier = pltpu.get_barrier_semaphore()
    for neighbour in (after, before, up, dn, across, twin):
        pl.semaphore_signal(barrier, inc=1, device_id=neighbour, device_id_type=MESH)
    pl.semaphore_wait(barrier, 6)

    def remote(src, dst, send, recv, to):
        return pltpu.make_async_remote_copy(
            src_ref=src, dst_ref=dst, send_sem=send, recv_sem=recv, device_id=to, device_id_type=MESH
        )

    def pp_copy(t, src, j, to):
        return remote(
            src.at[:, pl.ds(pl.multiple_of(j * cw, cw), cw)], arr.at[t], pp_send, pp_recv.at[t], to
        )

    def start_pp(j, carry):
        pp_copy(j, section_out, j, after).start()
        pp_copy(CHUNKS + j, cot_next, j, before).start()
        return carry

    lax.fori_loop(0, CHUNKS, start_pp, 0)

    def shared(src, dst, at):
        return remote(src, dst, core_send.at[at], core_recv.at[at], twin)

    shares = [
        shared(w_gate.at[0], gate_up.at[:, pl.ds(own_lane, unit)], 0),
        shared(w_up.at[0], gate_up.at[:, pl.ds(pl.multiple_of(units + core * unit, unit), unit)], 1),
        shared(w_down.at[0], down.at[pl.ds(own_lane, unit)], 2),
        shared(saved_gate.at[:, 1 - core], held_gate.at[:, :, pl.ds(own_lane, unit)], 3),
        shared(saved_up.at[:, 1 - core], held_up.at[:, :, pl.ds(own_lane, unit)], 4),
    ]
    for one in shares:
        one.start()

    first = lax.broadcasted_iota(jnp.int32, (count, count), 0)
    second = lax.broadcasted_iota(jnp.int32, (count, count), 1)
    diagonal = first == second
    ones = jnp.ones((count, count), bf16)

    def places(routes, m):
        along = jnp.broadcast_to(routes[...].astype(f32), (count, count))
        down_rows = jnp.dot(jnp.where(diagonal, along, 0.0).astype(bf16), ones, preferred_element_type=f32)
        same = along == down_rows
        earlier = jnp.where(same & (first < second), 1.0, 0.0)
        place_along = along * cap + jnp.sum(earlier, axis=0, keepdims=True)
        chosen = place_along == first.astype(f32)
        pick[m] = jnp.where(chosen, 1.0, 0.0).astype(bf16)
        earlier = jnp.where(same & (second < first), 1.0, 0.0)
        place_down = down_rows * cap + jnp.sum(earlier, axis=1, keepdims=True)
        unpick[m] = jnp.where(place_down == second.astype(f32), 1.0, 0.0).astype(bf16)
        return chosen

    chosen = places(routes_fwd, 0)
    slot_gate = jnp.sum(jnp.where(chosen, jnp.broadcast_to(gates_fwd[...], (count, count)), 0.0), axis=1, keepdims=True)
    gate_out[...] = jnp.broadcast_to(slot_gate, (count, 128)).reshape(EXPERTS, cap, 128)
    row_gate[0, plane] = gate_out[plane]
    gate_copy = remote(gate_out.at[other], row_gate.at[0, plane], gate_send_sem, gate_recv_sem, across)
    gate_copy.start()
    row_gate[1] = jnp.ones((EXPERTS, cap, 128), f32)
    factor[0] = jnp.ones((count, 128), f32)
    chosen = places(routes_bwd, 1)
    slot_gate = jnp.sum(jnp.where(chosen, jnp.broadcast_to(gates_bwd[...], (count, count)), 0.0), axis=1, keepdims=True)
    factor[1] = jnp.broadcast_to(slot_gate, (count, 128))
    squares[...] = jnp.zeros_like(squares)
    act[...] = jnp.zeros_like(act)
    back_act[...] = jnp.zeros_like(back_act)

    def columns(j):
        return pl.ds(pl.multiple_of(j * cw, cw), cw)

    def cross(t):
        return remote(disp.at[t, other], rows.at[t, plane, y], x_send, x_recv.at[t], across)

    def crossed(t):
        return remote(disp.at[t, other], rows.at[t, other, y], x_send, x_recv.at[t], across)

    def ring_copy(t, side, at, to, sem):
        return remote(rows.at[t, side, at], rows.at[t, side, at], y_send.at[sem], y_recv.at[t, sem], to)

    def dispatch(t):
        m = t // CHUNKS
        pp_copy(t, section_out, 0, after).wait_recv()
        moved = jnp.dot(pick[m], arr[t], preferred_element_type=f32) * factor[m][:, 0:1]
        disp[t] = moved.astype(bf16).reshape(EXPERTS, cap, cw)
        cross(t).start()
        rows[t, plane, y] = disp[t, plane]
        ring_copy(t, plane, y, up, plane).start()
        ring_copy(t, plane, y, dn, 2 + plane).start()

    def spread(t):
        crossed(t).wait_recv()
        ring_copy(t, other, y, up, other).start()
        ring_copy(t, other, y, dn, 2 + other).start()

    def forward(t):
        ring_copy(t, 0, y_down, up, 0).wait_recv()
        ring_copy(t, 0, y_down, up, 4).start()
        ring_copy(t, 1, y_up, dn, 3).wait_recv()
        ring_copy(t, 1, y_up, dn, 5).start()

    def gathered(t):
        ring_copy(t, 1, y_down, up, 1).wait_recv()
        ring_copy(t, 0, y_up, dn, 2).wait_recv()
        ring_copy(t, 0, y_far, up, 4).wait_recv()
        ring_copy(t, 1, y_far, dn, 5).wait_recv()

    def multiply_fwd(t):
        @pl.when(t == 0)
        def _():
            for at in (0, 1):
                loads[at].wait()
                shares[at].wait_recv()

        floats = rows[t].reshape(total, cw).astype(f32)
        squared = floats * floats
        lanes = squared[:, 0:128]
        for k in range(1, cw // 128):
            lanes = lanes + squared[:, k * 128 : (k + 1) * 128]
        squares[...] += lanes
        left = (floats * norm_gain[:, columns(t)]).astype(bf16)
        act[...] += jnp.dot(left, gate_up[columns(t), :], preferred_element_type=f32)

        @pl.when(t == CHUNKS - 1)
        def _():
            mean = jnp.sum(squares[...], axis=1, keepdims=True) * (1.0 / width)
            scale = lax.rsqrt(mean + EPS)
            gate_act = act[:, 0:units] * scale
            up_act = act[:, units : 2 * units] * scale
            inner[...] = (gate_act * jax.nn.sigmoid(gate_act) * up_act).astype(bf16)

    def multiply_bwd(t):
        j = t - CHUNKS

        @pl.when(j == 0)
        def _():
            for at in (2, 3, 4):
                loads[at].wait()
                shares[at].wait_recv()

        back_act[...] += lax.dot_general(
            rows[t].reshape(total, cw), down[:, columns(j)], (((1,), (1,)), ((), ())), preferred_element_type=f32
        )

        @pl.when(j == CHUNKS - 1)
        def _():
            inner_grad = back_act[...]
            gate_act = held_gate[...].reshape(total, units).astype(f32)
            up_act = held_up[...].reshape(total, units).astype(f32)
            sigma = jax.nn.sigmoid(gate_act)
            gate_grad = inner_grad * up_act * sigma * (1.0 + gate_act * (1.0 - sigma))
            back_inner[:, 0:units] = gate_grad.astype(bf16)
            back_inner[:, units : 2 * units] = (inner_grad * gate_act * sigma).astype(bf16)

    def far_copy(u, way, to):
        return remote(far_send.at[u, way], far_recv.at[u, way], far_send_sem.at[way], far_recv_sem.at[u, way], to)

    def near_copy(u, way, to):
        return remote(near_send.at[u, way], near_recv.at[u, way], near_send_sem.at[way], near_recv_sem.at[u, way], to)

    def produce(u):
        @pl.when(u < CHUNKS)
        def _():
            value = jnp.dot(inner[...], down[:, columns(u)], preferred_element_type=f32)
            part[u] = value.reshape(EXPERTS, RING, cap, cw)

        @pl.when(u >= CHUNKS)
        def _():
            value = lax.dot_general(
                back_inner[...],
                gate_up[columns(u - CHUNKS), :],
                (((1,), (1,)), ((), ())),
                preferred_element_type=f32,
            )
            part[u] = value.reshape(EXPERTS, RING, cap, cw)

        far_send[u, 0] = part[u, 0, y_far].astype(bf16)
        far_send[u, 1] = part[u, 1, y_far].astype(bf16)
        far_copy(u, 0, up).start()
        far_copy(u, 1, dn).start()

    def add_far(u):
        near_send[u, 0, 1] = part[u, 1, y_up].astype(bf16)
        near_send[u, 1, 0] = part[u, 0, y_down].astype(bf16)
        far_copy(u, 0, up).wait_recv()
        near_send[u, 0, 0] = (part[u, 0, y_up] + far_recv[u, 0].astype(f32)).astype(bf16)
        near_copy(u, 0, up).start()
        far_copy(u, 1, dn).wait_recv()
        near_send[u, 1, 1] = (part[u, 1, y_down] + far_recv[u, 1].astype(f32)).astype(bf16)
        near_copy(u, 1, dn).start()

    def home_copy(u, at):
        return remote(home_send.at[u], home.at[u, at], home_send_sem, home_recv_sem.at[u], across)

    def finish(u):
        m = u // CHUNKS
        near_copy(u, 0, up).wait_recv()
        near_copy(u, 1, dn).wait_recv()

        @pl.when(u == 0)
        def _():
            remote(gate_out.at[other], row_gate.at[0, other], gate_send_sem, gate_recv_sem, across).wait_recv()

        keep = jnp.where(m == 0, 1.0, 0.0)

        def summed(side):
            value = part[u, side, y] + near_recv[u, 0, side].astype(f32) + near_recv[u, 1, side].astype(f32)
            return (rows[u, side, y].astype(f32) * keep + value * row_gate[m, side][:, 0:1]).astype(bf16)

        home_send[u] = summed(other)
        home_copy(u, plane).start()
        home[u, plane] = summed(plane)

    def out_copy(u, out, j):
        return pltpu.make_async_copy(out_buf.at[u], out.at[:, columns(j)], out_sem)

    def deliver(u):
        home_copy(u, other).wait_recv()
        back = jnp.dot(unpick[u // CHUNKS], home[u].reshape(count, cw), preferred_element_type=f32)
        out_buf[u] = back.astype(bf16)

        @pl.when(u < CHUNKS)
        def _():
            out_copy(u, result, u).start()

        @pl.when(u >= CHUNKS)
        def _():
            out_copy(u, grad_in, u - CHUNKS).start()

    def at_step(i, behind, action):
        t = i - behind

        @pl.when((t >= 0) & (t < steps))
        def _():
            action(t)

    def gather_multiply(t):
        gathered(t)

        @pl.when(t < CHUNKS)
        def _():
            multiply_fwd(t)

        @pl.when(t >= CHUNKS)
        def _():
            multiply_bwd(t)

    def step(i, carry):
        at_step(i, 0, dispatch)
        at_step(i, 1, spread)
        at_step(i, 2, forward)
        at_step(i, 3, gather_multiply)
        at_step(i, START, produce)
        at_step(i, START + 1, add_far)
        at_step(i, START + 2, finish)
        at_step(i, START + 3, deliver)
        return carry

    lax.fori_loop(0, START + steps + 3, step, 0)

    for one in shares:
        one.wait_send()
    gate_copy.wait_send()
    pltpu.make_async_copy(arr, arr, pp_send).wait()
    narrow = rows.at[:, 0, 0]
    pltpu.make_async_copy(narrow, narrow, x_send).wait()
    for at in range(6):
        pltpu.make_async_copy(narrow, narrow, y_send.at[at]).wait()
    for way in range(2):
        pltpu.make_async_copy(narrow, narrow, far_send_sem.at[way]).wait()
        pltpu.make_async_copy(arr, arr, near_send_sem.at[way]).wait()
    pltpu.make_async_copy(narrow, narrow, home_send_sem).wait()
    pltpu.make_async_copy(arr, arr, out_sem).wait()


def local(
    section_out,
    routes_fwd,
    gates_fwd,
    cot_next,
    routes_bwd,
    gates_bwd,
    norm_gain,
    saved_gate,
    saved_up,
    w_gate,
    w_up,
    w_down,
):
    count, width = section_out.shape
    cap = count // EXPERTS
    unit = w_gate.shape[2]
    units = unit * CORES
    groups = EXPERTS * RING
    total = groups * cap
    cw = width // CHUNKS
    steps = 2 * CHUNKS
    held = (groups, CORES, cap, unit)
    f32, bf16 = jnp.float32, jnp.bfloat16
    vmem = pl.BlockSpec(memory_space=pltpu.VMEM)
    hbm = pl.BlockSpec(memory_space=pl.ANY)
    dma = pltpu.SemaphoreType.DMA
    return pl.pallas_call(
        kernel,
        out_shape=[jax.ShapeDtypeStruct((count, width), bf16)] * 2,
        in_specs=[hbm, hbm, vmem, vmem, vmem, vmem, vmem] + [hbm] * 5,
        out_specs=[hbm, hbm],
        scratch_shapes=[
            pltpu.VMEM((steps, count, cw), bf16),
            pltpu.VMEM((steps, EXPERTS, cap, cw), bf16),
            pltpu.VMEM((steps, EXPERTS, RING, cap, cw), bf16),
            pltpu.VMEM((width, 2 * units), bf16),
            pltpu.VMEM((units, width), bf16),
            pltpu.VMEM((groups, cap, units), bf16),
            pltpu.VMEM((groups, cap, units), bf16),
            pltpu.VMEM((2, count, count), bf16),
            pltpu.VMEM((2, count, count), bf16),
            pltpu.VMEM((2, count, 128), f32),
            pltpu.VMEM((2, EXPERTS, cap, 128), f32),
            pltpu.VMEM((EXPERTS, cap, 128), f32),
            pltpu.VMEM((total, 2 * units), f32),
            pltpu.VMEM((total, 128), f32),
            pltpu.VMEM((total, units), bf16),
            pltpu.VMEM((total, units), f32),
            pltpu.VMEM((total, 2 * units), bf16),
            pltpu.VMEM((steps, EXPERTS, RING, cap, cw), f32),
            pltpu.VMEM((steps, 2, cap, cw), bf16),
            pltpu.VMEM((steps, 2, cap, cw), bf16),
            pltpu.VMEM((steps, 2, EXPERTS, cap, cw), bf16),
            pltpu.VMEM((steps, 2, EXPERTS, cap, cw), bf16),
            pltpu.VMEM((steps, cap, cw), bf16),
            pltpu.VMEM((steps, EXPERTS, cap, cw), bf16),
            pltpu.VMEM((steps, count, cw), bf16),
            dma((5,)),
            dma((5,)),
            dma((5,)),
            dma,
            dma((steps,)),
            dma,
            dma((steps,)),
            dma((6,)),
            dma((steps, 6)),
            dma((2,)),
            dma((steps, 2)),
            dma((2,)),
            dma((steps, 2)),
            dma,
            dma((steps,)),
            dma,
            dma,
            dma,
        ],
        compiler_params=pltpu.CompilerParams(
            collective_id=0, has_side_effects=True, vmem_limit_bytes=56 * 1024 * 1024
        ),
        cost_estimate=pl.CostEstimate(
            flops=12 * total * width * units, bytes_accessed=16 * 1024 * 1024, transcendentals=2 * total * units
        ),
        name="relay_step",
    )(
        section_out,
        cot_next,
        routes_fwd.reshape(1, count),
        gates_fwd.reshape(1, count),
        routes_bwd.reshape(1, count),
        gates_bwd.reshape(1, count),
        norm_gain,
        saved_gate.reshape(held),
        saved_up.reshape(held),
        w_gate,
        w_up,
        w_down,
    )


def solution(mesh):
    in_specs = (
        P(("pp", "ep"), None),
        P(("pp", "ep"), None),
        P(("pp", "ep"), None),
        P(("pp", "ep"), None),
        P(("pp", "ep"), None),
        P(("pp", "ep"), None),
        P("pp", None),
        P("pp", None, "ep"),
        P("pp", None, "ep"),
        P("pp", None, "ep"),
        P("pp", None, "ep"),
        P("pp", "ep", None),
    )
    out_specs = (P(("pp", "ep"), None), P(("pp", "ep"), None))

    def whole(*args):
        first, second = jax.shard_map(
            local, mesh=mesh, in_specs=in_specs, out_specs=out_specs, check_vma=False
        )(*args)
        return first, second

    return whole
```

time: 272 us -> 110 us (0.40)
  the two profiles are of different devices: /device:TPU:25 before, /device:TPU:4 now
where the time goes in v1:
time: 110 us
  Pallas kernels  107 us (97%)
  local copies, waits for them, and re-layouts  2.64 us (2%)
    pallas_call x1, Pallas kernels, local(): pl.pallas_call(kernel, out_shape=[jax.ShapeDtypeStruct((count, width), bf...  107 us
    unnamed x4, local copies, waits for them, and re-layouts  2.64 us

profile of v1, /device:TPU:4, one launch (start us, length us, event | category | flops | bytes accessed | tf_op | source)
XLA Modules:
  0.0 110.3 jit_solution(2303266433008749348)
XLA Ops:
  0.6 107.0 %relay_step.1 = (bf16[64,3584]{1,0:T(8,128)(2,1)}, bf16[64,3584]{1,0:T(8,128)(2,1)}) custom-call(bf16[64,3584]{1,0:T(8,128)(2,1)} %section_out.1, bf16[64,3584]{1,0:T(8,128)(2,1)} %cot_next.1, s32[1,64]{1,0:T(1,128)} %bitcast.8, f32[1,64]{1,0:T(1,128)} %bitcast.9, s32[1,64]{1,0:T(1,128)} %bitcast.10, f32[1,64]{1,0:T(1,128)} %bitcast.11, ...), custom_call_target="tpu_custom_call" | custom-call | flops 2818572288 | bytes 16777216 | tf_op jit(solution)/shard_map/relay_step/pallas_call | solution.py:426
  107.6 0.0 copy-start
  107.6 1.9 %copy.16 = bf16[64,3584]{1,0:T(8,128)(2,1)} copy(bf16[64,3584]{1,0:T(8,128)(2,1)} %get-tuple-element.4) | data formatting | bytes 917504
  109.5 0.0 copy-done
  109.5 0.8 copy.17
Async XLA Ops:
  107.6 1.9 %copy-start = (bf16[64,3584]{1,0:T(8,128)(2,1)S(1)}, bf16[64,3584]{1,0:T(8,128)(2,1)}, u32[]{:S(2)}) copy-start(bf16[64,3584]{1,0:T(8,128)(2,1)} %get-tuple-element.5) | copy-start | bytes 1376260

commit v2 on v0

v2 whole, which is shorter than its diff:
```python
import jax
import jax.numpy as jnp
from jax import lax
from jax.experimental import pallas as pl
from jax.experimental.pallas import tpu as pltpu
from jax.sharding import PartitionSpec as P

EXPERTS = 2
RING = 4
CORES = 2
LAYERS = 16
EPS = 1e-06
CHUNKS = 7
MESH = pl.DeviceIdType.MESH
TWIN_AT = 2
FWD_AT = 4
SPREAD = 1
FORWARD = 2
BWD_MULTIPLY_AT = 3
FWD_MULTIPLY_AT = 8
BWD_INNER_AT = 10
BWD_SUM_AT = (10, 12, 14, 18)
FWD_SUM_AT = (15, 18)
FWD, BWD, RELAY = 0, 1, 2


def kernel(
    section_out,
    cot_next,
    routes_fwd,
    gates_fwd,
    routes_bwd,
    gates_bwd,
    norm_gain,
    saved_gate,
    saved_up,
    w_gate,
    w_up,
    w_down,
    result,
    grad_in,
    leaving,
    arr,
    disp,
    rows_fwd,
    rows_bwd,
    gate_up,
    down,
    held_gate,
    held_up,
    pick,
    unpick,
    factor,
    act,
    squares,
    inner_send,
    inner,
    pair_grad,
    grad_send,
    grad_recv,
    inner_grad,
    both_grad,
    part_fwd,
    part_bwd,
    pair_send,
    pair_recv,
    far_send,
    far_recv,
    side_send,
    side_recv,
    own_send,
    own_recv,
    sums,
    out_buf,
    leaving_sem,
    load_sem,
    core_send,
    core_recv,
    pp_send,
    pp_recv,
    relay_send,
    x_send,
    x_recv,
    fwd_send,
    fwd_recv,
    bwd_send,
    bwd_recv,
    down_send,
    down_recv,
    down_core_send,
    down_core_recv,
    swap_send,
    swap_recv,
    pair_send_sem,
    pair_recv_sem,
    far_send_sem,
    far_recv_sem,
    side_send_sem,
    side_recv_sem,
    own_send_sem,
    own_recv_sem,
    out_sem,
    ready,
):
    count = section_out.shape[0]
    width = section_out.shape[1]
    cap = count // EXPERTS
    unit = w_gate.shape[2]
    units = unit * CORES
    cw = width // CHUNKS
    total = RING * count
    f32, bf16 = jnp.float32, jnp.bfloat16

    me_pp = lax.axis_index("pp")
    me = lax.axis_index("ep")
    n_pp = lax.axis_size("pp")
    layers = min(LAYERS, n_pp // 2)
    z = me_pp % layers
    z_base = me_pp - z
    wraps_up = (z + 1) // layers
    wraps_down = 1 - (z + layers - 1) // layers
    on_edge = (z == 0) | (z == layers - 1)
    plane = me // (RING * CORES)
    other = 1 - plane
    y = (me // CORES) % RING
    core = me % CORES
    half = y // 2
    side = y % 2
    y_a = y + 1 - 2 * side
    y_b = RING - 1 - y
    y_far = (y + 2) % RING

    def in_ring(at):
        return {"ep": plane * (RING * CORES) + at * CORES + core}

    chip_a = in_ring(y_a)
    chip_b = in_ring(y_b)
    across = {"ep": other * (RING * CORES) + y * CORES + core}
    across_a = {"ep": other * (RING * CORES) + y_a * CORES + core}
    across_b = {"ep": other * (RING * CORES) + y_b * CORES + core}
    twin = {"ep": plane * (RING * CORES) + y * CORES + (1 - core)}
    above = {"pp": z_base + (z + 1) % layers}
    below = {"pp": z_base + (z + layers - 1) % layers}
    mirror = {"pp": (me_pp + layers) % n_pp}

    barrier = pltpu.get_barrier_semaphore()

    def greet(**device):
        pl.semaphore_signal(barrier, inc=1, device_id=device, device_id_type=MESH)

    for at_plane, at_y in ((plane, y_a), (plane, y_b), (other, y), (other, y_a), (other, y_b)):
        greet(ep=at_plane * (RING * CORES) + at_y * CORES)
    pl.when(core == 1)(lambda: greet(ep=me - core))
    for section in (above, below, mirror):
        greet(pp=section["pp"], ep=me - core + 1)

    def tell(at):
        pl.semaphore_signal(ready.at[at], inc=1, device_id=twin, device_id_type=MESH)

    def columns(j):
        return pl.ds(pl.multiple_of(j * cw, cw), cw)

    def load_down(j):
        return pltpu.make_async_copy(w_down.at[0, :, columns(j)], down.at[j, core], load_sem.at[2])

    def load_rows(src, m, j):
        return pltpu.make_async_copy(src.at[:, columns(j)], leaving.at[m, j], leaving_sem.at[m])

    def start_loads(j, carry):
        load_rows(cot_next, BWD, j).start()
        load_rows(section_out, FWD, j).start()
        load_down(j).start()
        return carry

    lax.fori_loop(0, CHUNKS, start_loads, 0)
    loads = {}
    for at, (src, dst) in enumerate(
        [
            (w_gate.at[0], gate_up.at[core]),
            (w_up.at[0], gate_up.at[CORES + core]),
            (down.at[:, core], down.at[:, core]),
            (saved_gate.at[0, :, core], held_gate.at[core, :, 0]),
            (saved_gate.at[1, :, core], held_gate.at[core, :, 1]),
            (saved_up.at[0, :, core], held_up.at[core, :, 0]),
            (saved_up.at[1, :, core], held_up.at[core, :, 1]),
        ]
    ):
        loads[at] = pltpu.make_async_copy(src, dst, load_sem.at[at])
    for at in (0, 1, 3, 4, 5, 6):
        loads[at].start()
    @pl.when(core == 0)
    def _():
        pl.semaphore_wait(barrier, 5 * CORES + 1)
        tell(0)

    @pl.when(core == 1)
    def _():
        pl.semaphore_wait(ready.at[0], 1)

    loads[2].wait()

    def remote(src, dst, send, recv, to):
        return pltpu.make_async_remote_copy(
            src_ref=src, dst_ref=dst, send_sem=send, recv_sem=recv, device_id=to, device_id_type=MESH
        )

    def pp_copy(m, at, j, to):
        return remote(leaving.at[m, j], arr.at[at, j], pp_send, pp_recv.at[at, j], to)

    def down_copy(j):
        return remote(down.at[j, core], down.at[j, CORES + core], down_send, down_recv.at[j], chip_b)

    def start_down(j, carry):
        down_copy(j).start()
        return carry

    lax.fori_loop(0, CHUNKS, start_down, 0)

    def shared(src, dst, at):
        return remote(src, dst, core_send.at[at], core_recv.at[at], twin)

    shares = [
        shared(gate_up.at[core], gate_up.at[core], 0),
        shared(gate_up.at[CORES + core], gate_up.at[CORES + core], 1),
        shared(down.at[:, core], down.at[:, core], 2),
        shared(saved_gate.at[0, :, 1 - core], held_gate.at[core, :, 0], 3),
        shared(saved_gate.at[1, :, 1 - core], held_gate.at[core, :, 1], 4),
        shared(saved_up.at[0, :, 1 - core], held_up.at[core, :, 0], 5),
        shared(saved_up.at[1, :, 1 - core], held_up.at[core, :, 1], 6),
    ]
    for at in (2, 0, 1, 3, 4, 5, 6):
        if at < 2:
            loads[at].wait()
        shares[at].start()

    @pl.when(core == 1)
    def _():
        pl.semaphore_wait(barrier, 3 * CORES)
        tell(1)

    @pl.when(core == 0)
    def _():
        pl.semaphore_wait(ready.at[1], 1)

    for m in (BWD, FWD):
        pltpu.make_async_copy(leaving.at[m], leaving.at[m], leaving_sem.at[m]).wait()

    def start_first(j, carry):
        pp_copy(BWD, BWD + wraps_down, j, below).start()
        pp_copy(FWD, FWD + 2 * wraps_up, j, above).start()
        return carry

    lax.fori_loop(0, CHUNKS, start_first, 0)

    first = lax.broadcasted_iota(jnp.int32, (count, count), 0)
    second = lax.broadcasted_iota(jnp.int32, (count, count), 1)
    diagonal = first == second
    ones = jnp.ones((count, count), bf16)

    def places(routes, m):
        along = jnp.broadcast_to(routes[...].astype(f32), (count, count))
        down_rows = jnp.dot(jnp.where(diagonal, along, 0.0).astype(bf16), ones, preferred_element_type=f32)
        same = along == down_rows
        earlier = jnp.where(same & (first < second), 1.0, 0.0)
        place_along = along * cap + jnp.sum(earlier, axis=0, keepdims=True)
        chosen = place_along == first.astype(f32)
        pick[m] = jnp.where(chosen, 1.0, 0.0).astype(bf16)
        earlier = jnp.where(same & (second < first), 1.0, 0.0)
        place_down = down_rows * cap + jnp.sum(earlier, axis=1, keepdims=True)
        unpick[m] = jnp.where(place_down == second.astype(f32), 1.0, 0.0).astype(bf16)
        return chosen

    for m, routes, gates in ((BWD, routes_bwd, gates_bwd), (FWD, routes_fwd, gates_fwd)):
        chosen = places(routes, m)
        along = jnp.broadcast_to(gates[...], (count, count))
        slot_gate = jnp.sum(jnp.where(chosen, along, 0.0), axis=1, keepdims=True)
        factor[m] = jnp.broadcast_to(slot_gate, (count, 128))
    squares[...] = jnp.zeros_like(squares)
    act[...] = jnp.zeros_like(act)
    pair_grad[...] = jnp.zeros_like(pair_grad)

    def relay(j):
        @pl.when(on_edge)
        def _():
            pp_copy(FWD, RELAY, j, above).wait_recv()
            remote(arr.at[RELAY, j], arr.at[wraps_up, j], relay_send, pp_recv.at[wraps_up, j], mirror).start()

    def down_twin(j):
        down_copy(j).wait_recv()
        mine = down.at[j, CORES + core]
        remote(mine, mine, down_core_send, down_core_recv.at[j], twin).start()

    def cross(m, rows, at, j, sender):
        return remote(disp.at[m, j, other], rows.at[j, at, sender], x_send.at[m], x_recv.at[m, j], across)

    def bwd_copy(j, expert):
        mine = rows_bwd.at[j, side, expert]
        return remote(mine, mine, bwd_send.at[expert], bwd_recv.at[j, expert], chip_a)

    def bwd_arrival(j, expert):
        theirs = rows_bwd.at[j, 1 - side, expert]
        return remote(theirs, theirs, bwd_send.at[expert], bwd_recv.at[j, expert], chip_a)

    def dispatch_bwd(j):
        pp_copy(BWD, BWD, j, below).wait_recv()
        moved = jnp.dot(pick[BWD], arr[BWD, j], preferred_element_type=f32) * factor[BWD][:, 0:1]
        disp[BWD, j] = moved.astype(bf16).reshape(EXPERTS, cap, cw)
        cross(BWD, rows_bwd, side, j, plane).start()
        rows_bwd[j, side, plane] = disp[BWD, j, plane]
        bwd_copy(j, plane).start()

    def spread_bwd(j):
        cross(BWD, rows_bwd, side, j, other).wait_recv()
        bwd_copy(j, other).start()

    def fwd_copy(j, at, expert, to, sem):
        mine = rows_fwd.at[j, at, expert]
        return remote(mine, mine, fwd_send.at[sem], fwd_recv.at[j, sem], to)

    def pass_copy(j, at):
        block = rows_fwd.at[j, at]
        return remote(block, block, fwd_send.at[4], fwd_recv.at[j, 4], chip_a)

    def dispatch_fwd(j):
        pp_copy(FWD, FWD, j, above).wait_recv()
        moved = jnp.dot(pick[FWD], arr[FWD, j], preferred_element_type=f32)
        disp[FWD, j] = moved.astype(bf16).reshape(EXPERTS, cap, cw)
        cross(FWD, rows_fwd, y, j, plane).start()
        rows_fwd[j, y, plane] = disp[FWD, j, plane]
        fwd_copy(j, y, plane, chip_b, 2 + plane).start()
        fwd_copy(j, y, plane, chip_a, plane).start()

    def spread_fwd(j):
        cross(FWD, rows_fwd, y, j, other).wait_recv()
        fwd_copy(j, y, other, chip_b, 2 + other).start()
        fwd_copy(j, y, other, chip_a, other).start()

    def forward_fwd(j):
        for expert in range(EXPERTS):
            fwd_copy(j, y_b, expert, chip_b, 2 + expert).wait_recv()
        pass_copy(j, y_b).start()

    def wait_loads(which):
        for at in which:
            if at > 2:
                loads[at].wait()
            shares[at].wait_recv()

    def both_weights(j):
        return jnp.concatenate([gate_up[at, columns(j), :] for at in range(2 * CORES)], axis=1)

    def all_units(held):
        return jnp.concatenate([held[at].reshape(total, unit) for at in range(CORES)], axis=1).astype(f32)

    def grad_swap():
        return remote(grad_send, grad_recv, swap_send.at[BWD], swap_recv.at[BWD], chip_b)

    def inner_swap():
        return remote(
            inner_send, inner.at[:, :, units : 2 * units], swap_send.at[FWD], swap_recv.at[FWD], chip_b
        )

    def multiply_bwd(j):
        @pl.when(j == 0)
        def _():
            wait_loads((2,))

        for expert in range(EXPERTS):
            bwd_arrival(j, expert).wait_recv()
        theirs = down.at[j, CORES + 1 - core]
        remote(theirs, theirs, down_core_send, down_core_recv.at[j], twin).wait_recv()
        pair_grad[...] += lax.dot_general(
            rows_bwd[j].reshape(2 * count, cw),
            down[j].reshape(2 * units, cw),
            (((1,), (1,)), ((), ())),
            preferred_element_type=f32,
        )

        @pl.when(j == CHUNKS - 1)
        def _():
            grad_send[...] = pair_grad[:, units : 2 * units].astype(bf16).reshape(2, count, units)
            grad_swap().start()
            inner_grad[pl.ds(2 * half, 2)] = pair_grad[:, 0:units].reshape(2, count, units)

    def finish_inner_grad():
        wait_loads((3, 4, 5, 6))
        grad_swap().wait_recv()
        inner_grad[pl.ds(2 * (1 - half), 2)] = grad_recv[...].astype(f32)
        grad = inner_grad[...].reshape(total, units)
        gate_act = all_units(held_gate)
        up_act = all_units(held_up)
        sigma = jax.nn.sigmoid(gate_act)
        both_grad[:, 0:units] = (grad * up_act * sigma * (1.0 + gate_act * (1.0 - sigma))).astype(bf16)
        both_grad[:, units : 2 * units] = (grad * gate_act * sigma).astype(bf16)

    def multiply_fwd(j):
        @pl.when(j == 0)
        def _():
            wait_loads((0, 1))

        for expert in range(EXPERTS):
            fwd_copy(j, y_a, expert, chip_a, expert).wait_recv()
        pass_copy(j, y_far).wait_recv()
        floats = rows_fwd[j].reshape(total, cw).astype(f32)
        squared = floats * floats
        summed = squared[:, 0:128]
        for k in range(1, cw // 128):
            summed = summed + squared[:, k * 128 : (k + 1) * 128]
        squares[...] += summed
        left = (floats * norm_gain[:, columns(j)]).astype(bf16)
        act[...] += jnp.dot(left, both_weights(j), preferred_element_type=f32)

        @pl.when(j == CHUNKS - 1)
        def _():
            mean = jnp.sum(squares[...], axis=1, keepdims=True) * (1.0 / width)
            scale = lax.rsqrt(mean + EPS)
            gate_act = act[:, 0:units] * scale
            up_act = act[:, units : 2 * units] * scale
            value = (gate_act * jax.nn.sigmoid(gate_act) * up_act).astype(bf16).reshape(2, 2, count, units)
            for at in range(2):
                @pl.when(half == at)
                def _():
                    inner[:, :, 0:units] = value[at]
                    inner_send[...] = value[1 - at]
            inner_swap().start()

    def far_copy(j):
        return remote(far_send.at[j], far_recv.at[j], far_send_sem, far_recv_sem.at[j], chip_b)

    def side_copy(j, way, expert, sender, to):
        return remote(
            side_send.at[way, j, expert],
            side_recv.at[way, j, sender],
            side_send_sem.at[way],
            side_recv_sem.at[way, j, sender],
            to,
        )

    def own_copy(m, j):
        return remote(own_send.at[m, j], own_recv.at[m, j], own_send_sem.at[m], own_recv_sem.at[m, j], across)

    def produce_bwd(j):
        value = lax.dot_general(
            both_grad[...], both_weights(j), (((1,), (1,)), ((), ())), preferred_element_type=f32
        )
        part_bwd[j] = value.reshape(RING, EXPERTS, cap, cw)
        far_send[j] = part_bwd[j, y_far].astype(bf16)
        far_copy(j).start()
        own_send[BWD, j] = part_bwd[j, y, other].astype(bf16)
        own_copy(BWD, j).start()
        side_send[1, j] = part_bwd[j, y_b].astype(bf16)

    def send_side(j):
        side_copy(j, 1, plane, plane, chip_b).start()
        side_copy(j, 1, other, plane, across_b).start()

    def add_bwd(j):
        far_copy(j).wait_recv()
        side_send[0, j] = (part_bwd[j, y_a] + far_recv[j].astype(f32)).astype(bf16)
        side_copy(j, 0, plane, plane, chip_a).start()
        side_copy(j, 0, other, plane, across_a).start()

    def pair_copy(j, expert, sender, to):
        return remote(pair_send.at[j, expert], pair_recv.at[j, sender], pair_send_sem, pair_recv_sem.at[j, sender], to)

    def produce_fwd(j):
        @pl.when(j == 0)
        def _():
            inner_swap().wait_recv()

        value = jnp.dot(
            inner[...].reshape(2 * count, 2 * units), down[j].reshape(2 * units, cw), preferred_element_type=f32
        )
        part_fwd[j] = value.reshape(2, EXPERTS, cap, cw)
        pair_send[j] = part_fwd[j, 1 - side].astype(bf16)
        pair_copy(j, plane, plane, chip_a).start()
        pair_copy(j, other, plane, across_a).start()
        own_send[FWD, j] = part_fwd[j, side, other].astype(bf16)
        own_copy(FWD, j).start()

    def out_copy(m, out, j):
        return pltpu.make_async_copy(out_buf.at[m, j], out.at[:, columns(j)], out_sem.at[m])

    def deliver(m, out, j, slots):
        back = jnp.dot(unpick[m], slots.reshape(count, cw), preferred_element_type=f32)
        out_buf[m, j] = back.astype(bf16)
        out_copy(m, out, j).start()

    def finish_bwd(j):
        own_copy(BWD, j).wait_recv()
        for way, here, there in ((0, chip_a, across_a), (1, chip_b, across_b)):
            side_copy(j, way, plane, plane, here).wait_recv()
            side_copy(j, way, other, other, there).wait_recv()
        sums[plane] = part_bwd[j, y, plane]
        sums[other] = own_recv[BWD, j].astype(f32)
        value = sums[...] + side_recv[0, j].astype(f32) + side_recv[1, j].astype(f32)
        deliver(BWD, grad_in, j, value.astype(bf16))

    def finish_fwd(j):
        own_copy(FWD, j).wait_recv()
        pair_copy(j, plane, plane, chip_a).wait_recv()
        pair_copy(j, other, other, across_a).wait_recv()
        sums[plane] = part_fwd[j, side, plane]
        sums[other] = own_recv[FWD, j].astype(f32)
        value = (sums[...] + pair_recv[j].astype(f32)).reshape(count, cw) * factor[FWD][:, 0:1]
        deliver(FWD, result, j, (disp[FWD, j].astype(f32).reshape(count, cw) + value).astype(bf16))

    def at_step(i, start, action):
        j = i - start

        @pl.when((j >= 0) & (j < CHUNKS))
        def _():
            action(j)

    relay(0)

    def step(i, carry):
        at_step(i + 1, 1, lambda j: pl.when(j + 1 < CHUNKS)(lambda: relay(j + 1)))
        at_step(i, TWIN_AT, down_twin)
        at_step(i, 0, dispatch_bwd)
        at_step(i, FWD_AT, dispatch_fwd)
        at_step(i, SPREAD, spread_bwd)
        at_step(i, FWD_AT + SPREAD, spread_fwd)
        at_step(i, FWD_AT + FORWARD, forward_fwd)
        at_step(i, BWD_MULTIPLY_AT, multiply_bwd)
        at_step(i, FWD_MULTIPLY_AT, multiply_fwd)
        pl.when(i == BWD_INNER_AT)(finish_inner_grad)
        at_step(i, BWD_SUM_AT[0], produce_bwd)
        at_step(i, BWD_SUM_AT[1], add_bwd)
        at_step(i, BWD_SUM_AT[2], send_side)
        at_step(i, FWD_SUM_AT[0], produce_fwd)
        at_step(i, FWD_SUM_AT[1], finish_fwd)
        at_step(i, BWD_SUM_AT[3], finish_bwd)
        return carry

    lax.fori_loop(0, max(BWD_SUM_AT[3], FWD_SUM_AT[1]) + CHUNKS, step, 0)

    for one in shares:
        one.wait_send()
    grad_swap().wait_send()
    inner_swap().wait_send()

    def sent(ref, sem):
        pltpu.make_async_copy(ref, ref, sem).wait()

    sent(arr.at[0:2], pp_send)
    pl.when(on_edge)(lambda: sent(arr.at[0], relay_send))
    sent(down.at[:, 0], down_send)
    sent(down.at[:, 0], down_core_send)
    narrow = disp.at[0, :, 0]
    for m in range(2):
        sent(narrow, x_send.at[m])
        sent(narrow, bwd_send.at[m])
        sent(narrow, own_send_sem.at[m])
        sent(out_buf.at[m], out_sem.at[m])
        sent(side_send.at[m], side_send_sem.at[m])
    for at in range(4):
        sent(narrow, fwd_send.at[at])
    sent(pair_send, fwd_send.at[4])
    sent(pair_send, pair_send_sem)
    sent(far_send, far_send_sem)


def local(
    section_out,
    routes_fwd,
    gates_fwd,
    cot_next,
    routes_bwd,
    gates_bwd,
    norm_gain,
    saved_gate,
    saved_up,
    w_gate,
    w_up,
    w_down,
):
    count, width = section_out.shape
    cap = count // EXPERTS
    unit = w_gate.shape[2]
    units = unit * CORES
    total = RING * count
    cw = width // CHUNKS
    held = (EXPERTS, RING, CORES, cap, unit)
    f32, bf16 = jnp.float32, jnp.bfloat16
    vmem = pl.BlockSpec(memory_space=pltpu.VMEM)
    hbm = pl.BlockSpec(memory_space=pl.ANY)
    dma = pltpu.SemaphoreType.DMA
    block = (EXPERTS, cap, cw)
    return pl.pallas_call(
        kernel,
        out_shape=[jax.ShapeDtypeStruct((count, width), bf16)] * 2,
        in_specs=[hbm, hbm, vmem, vmem, vmem, vmem, vmem] + [hbm] * 5,
        out_specs=[hbm, hbm],
        scratch_shapes=[
            pltpu.VMEM((2, CHUNKS, count, cw), bf16),
            pltpu.VMEM((3, CHUNKS, count, cw), bf16),
            pltpu.VMEM((2, CHUNKS) + block, bf16),
            pltpu.VMEM((CHUNKS, RING) + block, bf16),
            pltpu.VMEM((CHUNKS, 2) + block, bf16),
            pltpu.VMEM((2 * CORES, width, unit), bf16),
            pltpu.VMEM((CHUNKS, 2 * CORES, unit, cw), bf16),
            pltpu.VMEM((CORES, RING, EXPERTS, cap, unit), bf16),
            pltpu.VMEM((CORES, RING, EXPERTS, cap, unit), bf16),
            pltpu.VMEM((2, count, count), bf16),
            pltpu.VMEM((2, count, count), bf16),
            pltpu.VMEM((2, count, 128), f32),
            pltpu.VMEM((total, 2 * units), f32),
            pltpu.VMEM((total, 128), f32),
            pltpu.VMEM((2, count, units), bf16),
            pltpu.VMEM((2, count, 2 * units), bf16),
            pltpu.VMEM((2 * count, 2 * units), f32),
            pltpu.VMEM((2, count, units), bf16),
            pltpu.VMEM((2, count, units), bf16),
            pltpu.VMEM((RING, count, units), f32),
            pltpu.VMEM((total, 2 * units), bf16),
            pltpu.VMEM((CHUNKS, 2) + block, f32),
            pltpu.VMEM((CHUNKS, RING) + block, f32),
            pltpu.VMEM((CHUNKS,) + block, bf16),
            pltpu.VMEM((CHUNKS,) + block, bf16),
            pltpu.VMEM((CHUNKS,) + block, bf16),
            pltpu.VMEM((CHUNKS,) + block, bf16),
            pltpu.VMEM((2, CHUNKS) + block, bf16),
            pltpu.VMEM((2, CHUNKS) + block, bf16),
            pltpu.VMEM((2, CHUNKS, cap, cw), bf16),
            pltpu.VMEM((2, CHUNKS, cap, cw), bf16),
            pltpu.VMEM(block, f32),
            pltpu.VMEM((2, CHUNKS, count, cw), bf16),
            dma((2,)),
            dma((7,)),
            dma((7,)),
            dma((7,)),
            dma,
            dma((3, CHUNKS)),
            dma,
            dma((2,)),
            dma((2, CHUNKS)),
            dma((5,)),
            dma((CHUNKS, 5)),
            dma((2,)),
            dma((CHUNKS, 2)),
            dma,
            dma((CHUNKS,)),
            dma,
            dma((CHUNKS,)),
            dma((2,)),
            dma((2,)),
            dma,
            dma((CHUNKS, EXPERTS)),
            dma,
            dma((CHUNKS,)),
            dma((2,)),
            dma((2, CHUNKS, EXPERTS)),
            dma((2,)),
            dma((2, CHUNKS)),
            dma((2,)),
            pltpu.SemaphoreType.REGULAR((2,)),
        ],
        compiler_params=pltpu.CompilerParams(
            collective_id=0, has_side_effects=True, vmem_limit_bytes=58 * 1024 * 1024
        ),
        cost_estimate=pl.CostEstimate(
            flops=12 * total * width * units, bytes_accessed=16 * 1024 * 1024, transcendentals=2 * total * units
        ),
        name="relay_step",
    )(
        section_out,
        cot_next,
        routes_fwd.reshape(1, count),
        gates_fwd.reshape(1, count),
        routes_bwd.reshape(1, count),
        gates_bwd.reshape(1, count),
        norm_gain,
        saved_gate.reshape(held),
        saved_up.reshape(held),
        w_gate,
        w_up,
        w_down,
    )


def solution(mesh):
    in_specs = (
        P(("pp", "ep"), None),
        P(("pp", "ep"), None),
        P(("pp", "ep"), None),
        P(("pp", "ep"), None),
        P(("pp", "ep"), None),
        P(("pp", "ep"), None),
        P("pp", None),
        P("pp", None, "ep"),
        P("pp", None, "ep"),
        P("pp", None, "ep"),
        P("pp", None, "ep"),
        P("pp", "ep", None),
    )
    out_specs = (P(("pp", "ep"), None), P(("pp", "ep"), None))

    def whole(*args):
        first, second = jax.shard_map(
            local, mesh=mesh, in_specs=in_specs, out_specs=out_specs, check_vma=False
        )(*args)
        return first, second

    return whole
```

time: 272 us -> 84.9 us (0.31)
  the two profiles are of different devices: /device:TPU:25 before, /device:TPU:4 now
where the time goes in v2:
time: 84.9 us; the launch traced here: 84.7 us
  Pallas kernels  81.4 us (96%)
  local copies, waits for them, and re-layouts  2.64 us (3%)
    pallas_call x1, Pallas kernels, local(): pl.pallas_call(kernel, out_shape=[jax.ShapeDtypeStruct((count, width), bf...  81.4 us
    unnamed x4, local copies, waits for them, and re-layouts  2.64 us

profile of v2, /device:TPU:4, one launch (start us, length us, event | category | flops | bytes accessed | tf_op | source)
XLA Modules:
  0.0 84.7 jit_solution(12053446513862861606)
XLA Ops:
  0.6 81.4 %relay_step.1 = (bf16[64,3584]{1,0:T(8,128)(2,1)}, bf16[64,3584]{1,0:T(8,128)(2,1)}) custom-call(bf16[64,3584]{1,0:T(8,128)(2,1)} %section_out.1, bf16[64,3584]{1,0:T(8,128)(2,1)} %cot_next.1, s32[1,64]{1,0:T(1,128)} %bitcast.8, f32[1,64]{1,0:T(1,128)} %bitcast.9, s32[1,64]{1,0:T(1,128)} %bitcast.10, f32[1,64]{1,0:T(1,128)} %bitcast.11, ...), custom_call_target="tpu_custom_call" | custom-call | flops 2818572288 | bytes 16777216 | tf_op jit(solution)/shard_map/relay_step/pallas_call | solution.py:590
  82.1 0.0 copy-start
  82.1 1.9 %copy.16 = bf16[64,3584]{1,0:T(8,128)(2,1)} copy(bf16[64,3584]{1,0:T(8,128)(2,1)} %get-tuple-element.4) | data formatting | bytes 917504
  84.0 0.0 copy-done
  84.0 0.8 copy.17
Async XLA Ops:
  82.1 1.9 %copy-start = (bf16[64,3584]{1,0:T(8,128)(2,1)S(1)}, bf16[64,3584]{1,0:T(8,128)(2,1)}, u32[]{:S(2)}) copy-start(bf16[64,3584]{1,0:T(8,128)(2,1)} %get-tuple-element.5) | copy-start | bytes 1376260

commit v3 on v2

--- a/solution.py
+++ b/solution.py
@@ -10,17 +10,18 @@
 CORES = 2
 LAYERS = 16
 EPS = 1e-06
-CHUNKS = 7
+CHUNKS = 4
 MESH = pl.DeviceIdType.MESH
-TWIN_AT = 2
-FWD_AT = 4
+RELAY_AT = 1
+TWIN_AT = 1
+FWD_AT = 2
 SPREAD = 1
 FORWARD = 2
-BWD_MULTIPLY_AT = 3
-FWD_MULTIPLY_AT = 8
-BWD_INNER_AT = 10
-BWD_SUM_AT = (10, 12, 14, 18)
-FWD_SUM_AT = (15, 18)
+BWD_MULTIPLY_AT = 2
+FWD_MULTIPLY_AT = 5
+BWD_INNER_AT = 6
+BWD_SUM_AT = (6, 8, 9, 11)
+FWD_SUM_AT = (9, 11)
 FWD, BWD, RELAY = 0, 1, 2
 
 
@@ -120,6 +121,7 @@
     wraps_up = (z + 1) // layers
     wraps_down = 1 - (z + layers - 1) // layers
     on_edge = (z == 0) | (z == layers - 1)
+    split_way = z == 0
     plane = me // (RING * CORES)
     other = 1 - plane
     y = (me // CORES) % RING
@@ -279,11 +281,15 @@
     act[...] = jnp.zeros_like(act)
     pair_grad[...] = jnp.zeros_like(pair_grad)
 
-    def relay(j):
-        @pl.when(on_edge)
-        def _():
-            pp_copy(FWD, RELAY, j, above).wait_recv()
-            remote(arr.at[RELAY, j], arr.at[wraps_up, j], relay_send, pp_recv.at[wraps_up, j], mirror).start()
+    def relay(j, m):
+        pp_copy(FWD, RELAY, j, above).wait_recv()
+        remote(arr.at[RELAY, j], arr.at[m, j], relay_send, pp_recv.at[m, j], mirror).start()
+
+    def relay_fwd(j):
+        pl.when(z == 0)(lambda: relay(j, FWD))
+
+    def relay_bwd(j):
+        pl.when(z == layers - 1)(lambda: relay(j, BWD))
 
     def down_twin(j):
         down_copy(j).wait_recv()
@@ -317,9 +323,9 @@
         mine = rows_fwd.at[j, at, expert]
         return remote(mine, mine, fwd_send.at[sem], fwd_recv.at[j, sem], to)
 
-    def pass_copy(j, at):
-        block = rows_fwd.at[j, at]
-        return remote(block, block, fwd_send.at[4], fwd_recv.at[j, 4], chip_a)
+    def pass_copy(j, at, expert, to):
+        block = rows_fwd.at[j, at, expert]
+        return remote(block, block, fwd_send.at[4], fwd_recv.at[j, 4 + expert], to)
 
     def dispatch_fwd(j):
         pp_copy(FWD, FWD, j, above).wait_recv()
@@ -336,9 +342,18 @@
         fwd_copy(j, y, other, chip_a, other).start()
 
     def forward_fwd(j):
-        for expert in range(EXPERTS):
-            fwd_copy(j, y_b, expert, chip_b, 2 + expert).wait_recv()
-        pass_copy(j, y_b).start()
+        fwd_copy(j, y_b, 0, chip_b, 2).wait_recv()
+        pass_copy(j, y_b, 0, chip_a).start()
+
+        @pl.when(split_way)
+        def _():
+            fwd_copy(j, y_a, 1, chip_a, 1).wait_recv()
+            pass_copy(j, y_a, 1, chip_b).start()
+
+        @pl.when(jnp.logical_not(split_way))
+        def _():
+            fwd_copy(j, y_b, 1, chip_b, 3).wait_recv()
+            pass_copy(j, y_b, 1, chip_a).start()
 
     def wait_loads(which):
         for at in which:
@@ -398,9 +413,18 @@
         def _():
             wait_loads((0, 1))
 
+        fwd_copy(j, y_a, 0, chip_a, 0).wait_recv()
+
+        @pl.when(split_way)
+        def _():
+            fwd_copy(j, y_b, 1, chip_b, 3).wait_recv()
+
+        @pl.when(jnp.logical_not(split_way))
+        def _():
+            fwd_copy(j, y_a, 1, chip_a, 1).wait_recv()
+
         for expert in range(EXPERTS):
-            fwd_copy(j, y_a, expert, chip_a, expert).wait_recv()
-        pass_copy(j, y_far).wait_recv()
+            pass_copy(j, y_far, expert, chip_a).wait_recv()
         floats = rows_fwd[j].reshape(total, cw).astype(f32)
         squared = floats * floats
         summed = squared[:, 0:128]
@@ -512,10 +536,11 @@
         def _():
             action(j)
 
-    relay(0)
+    relay_bwd(0)
 
     def step(i, carry):
-        at_step(i + 1, 1, lambda j: pl.when(j + 1 < CHUNKS)(lambda: relay(j + 1)))
+        at_step(i, -1, relay_bwd)
+        at_step(i, RELAY_AT, relay_fwd)
         at_step(i, TWIN_AT, down_twin)
         at_step(i, 0, dispatch_bwd)
         at_step(i, FWD_AT, dispatch_fwd)
@@ -587,7 +612,7 @@
     hbm = pl.BlockSpec(memory_space=pl.ANY)
     dma = pltpu.SemaphoreType.DMA
     block = (EXPERTS, cap, cw)
-    return pl.pallas_call(
+    first, second = pl.pallas_call(
         kernel,
         out_shape=[jax.ShapeDtypeStruct((count, width), bf16)] * 2,
         in_specs=[hbm, hbm, vmem, vmem, vmem, vmem, vmem] + [hbm] * 5,
@@ -636,7 +661,7 @@
             dma((2,)),
             dma((2, CHUNKS)),
             dma((5,)),
-            dma((CHUNKS, 5)),
+            dma((CHUNKS, 6)),
             dma((2,)),
             dma((CHUNKS, 2)),
             dma,
@@ -678,6 +703,37 @@
         w_down,
     )
 
+    pieces = 4
+
+    def settle(first, second, result, grad_in, held, sem):
+        parts = []
+        for m, (src, dst) in enumerate(((first, result), (second, grad_in))):
+            for at in range(pieces):
+                rows = pl.ds(at * (count // pieces), count // pieces)
+                parts.append(
+                    (
+                        pltpu.make_async_copy(src.at[rows], held.at[m, rows], sem.at[0, m, at]),
+                        pltpu.make_async_copy(held.at[m, rows], dst.at[rows], sem.at[1, m, at]),
+                    )
+                )
+        for come, _ in parts:
+            come.start()
+        for come, go in parts:
+            come.wait()
+            go.start()
+        for _, go in parts:
+            go.wait()
+
+    return pl.pallas_call(
+        settle,
+        out_shape=[jax.ShapeDtypeStruct((count, width), bf16)] * 2,
+        in_specs=[hbm, hbm],
+        out_specs=[hbm, hbm],
+        scratch_shapes=[pltpu.VMEM((2, count, width), bf16), dma((2, 2, pieces))],
+        compiler_params=pltpu.CompilerParams(vmem_limit_bytes=58 * 1024 * 1024),
+        name="settle",
+    )(first, second)
+
 
 def solution(mesh):
     in_specs = (

time: 84.9 us -> 79.2 us (0.933)
  the two profiles are of different devices: /device:TPU:4 before, /device:TPU:8 now
where the time goes in v3:
time: 79.2 us; the launch traced here: 78.9 us
  Pallas kernels  78.3 us (99%)
    pallas_call x1, Pallas kernels, local(): pl.pallas_call(kernel, out_shape=[jax.ShapeDtypeStruct((count, width), bf...  76.3 us
    pallas_call x1, Pallas kernels, local(): pl.pallas_call(settle, out_shape=[jax.ShapeDtypeStruct((count, width), bf...  2.04 us

profile of v3, /device:TPU:8, one launch (start us, length us, event | category | flops | bytes accessed | tf_op | source)
XLA Modules:
  0.0 78.9 jit_solution(3924980840509419616)
XLA Ops:
  0.6 76.3 %relay_step.1 = (bf16[64,3584]{1,0:T(8,128)(2,1)}, bf16[64,3584]{1,0:T(8,128)(2,1)}) custom-call(bf16[64,3584]{1,0:T(8,128)(2,1)} %section_out.1, bf16[64,3584]{1,0:T(8,128)(2,1)} %cot_next.1, s32[1,64]{1,0:T(1,128)} %bitcast.8, f32[1,64]{1,0:T(1,128)} %bitcast.9, s32[1,64]{1,0:T(1,128)} %bitcast.10, f32[1,64]{1,0:T(1,128)} %bitcast.11, ...), custom_call_target="tpu_custom_call" | custom-call | flops 2818572288 | bytes 16777216 | tf_op jit(solution)/shard_map/relay_step/pallas_call | solution.py:615
  76.9 2.0 %settle.1 = (bf16[64,3584]{1,0:T(8,128)(2,1)}, bf16[64,3584]{1,0:T(8,128)(2,1)}) custom-call(bf16[64,3584]{1,0:T(8,128)(2,1)} %get-tuple-element.4.first, bf16[64,3584]{1,0:T(8,128)(2,1)} %get-tuple-element.5.second), custom_call_target="tpu_custom_call" | custom-call | tf_op jit(solution)/shard_map/settle/pallas_call | solution.py:727

commit v4 on v3

--- a/solution.py
+++ b/solution.py
@@ -20,7 +20,7 @@
 BWD_MULTIPLY_AT = 2
 FWD_MULTIPLY_AT = 5
 BWD_INNER_AT = 6
-BWD_SUM_AT = (6, 8, 9, 11)
+BWD_SUM_AT = (6, 8, 8, 11)
 FWD_SUM_AT = (9, 11)
 FWD, BWD, RELAY = 0, 1, 2
 
@@ -541,12 +541,12 @@
     def step(i, carry):
         at_step(i, -1, relay_bwd)
         at_step(i, RELAY_AT, relay_fwd)
-        at_step(i, TWIN_AT, down_twin)
         at_step(i, 0, dispatch_bwd)
         at_step(i, FWD_AT, dispatch_fwd)
         at_step(i, SPREAD, spread_bwd)
         at_step(i, FWD_AT + SPREAD, spread_fwd)
         at_step(i, FWD_AT + FORWARD, forward_fwd)
+        at_step(i, TWIN_AT, down_twin)
         at_step(i, BWD_MULTIPLY_AT, multiply_bwd)
         at_step(i, FWD_MULTIPLY_AT, multiply_fwd)
         pl.when(i == BWD_INNER_AT)(finish_inner_grad)

time: 79.2 us -> 78.9 us (level)
  the two profiles are of different devices: /device:TPU:8 before, /device:TPU:2 now
where the time goes in v4:
time: 78.9 us; the launch traced here: 78.7 us
  Pallas kernels  78 us (99%)
    pallas_call x1, Pallas kernels, local(): pl.pallas_call(kernel, out_shape=[jax.ShapeDtypeStruct((count, width), bf...  76 us
    pallas_call x1, Pallas kernels, local(): pl.pallas_call(settle, out_shape=[jax.ShapeDtypeStruct((count, width), bf...  2.04 us

profile of v4, /device:TPU:2, one launch (start us, length us, event | category | flops | bytes accessed | tf_op | source)
XLA Modules:
  0.0 78.7 jit_solution(12168946565842359606)
XLA Ops:
  0.6 76.0 %relay_step.1 = (bf16[64,3584]{1,0:T(8,128)(2,1)}, bf16[64,3584]{1,0:T(8,128)(2,1)}) custom-call(bf16[64,3584]{1,0:T(8,128)(2,1)} %section_out.1, bf16[64,3584]{1,0:T(8,128)(2,1)} %cot_next.1, s32[1,64]{1,0:T(1,128)} %bitcast.8, f32[1,64]{1,0:T(1,128)} %bitcast.9, s32[1,64]{1,0:T(1,128)} %bitcast.10, f32[1,64]{1,0:T(1,128)} %bitcast.11, ...), custom_call_target="tpu_custom_call" | custom-call | flops 2818572288 | bytes 16777216 | tf_op jit(solution)/shard_map/relay_step/pallas_call | solution.py:615
  76.6 2.0 %settle.1 = (bf16[64,3584]{1,0:T(8,128)(2,1)}, bf16[64,3584]{1,0:T(8,128)(2,1)}) custom-call(bf16[64,3584]{1,0:T(8,128)(2,1)} %get-tuple-element.4.first, bf16[64,3584]{1,0:T(8,128)(2,1)} %get-tuple-element.5.second), custom_call_target="tpu_custom_call" | custom-call | tf_op jit(solution)/shard_map/settle/pallas_call | solution.py:727
